TPU v7x, 256 devices: a whole 4x4x8 slice. The times are simulated.
256 devices in a mesh: seq: 32 (over x, z), fsdp: 8 (over y, core).
Axes of the slice: x: 4, y: 4, z: 8, core: 2. Of those that a mesh axis runs over, the one named last changes fastest.
Arguments:
- frames: bfloat16 [8, 4096, 1536], P('fsdp', 'seq'), may hold values from -6 to 6
- lengths: int32 [8, 4], P('fsdp'), may hold values from 1 to 2048, 4096 in all within a row
- offsets: int32 [8, 33], P('fsdp'), may hold values from 0 to 4096, as said below
- w_in: bfloat16 [1536, 3072], P('fsdp'), may hold values from -0.15625 to 0.15625
- kernel: float32 [31, 1536], replicated, may hold values from -1 to 1
- cotangent: bfloat16 [8, 8192, 1536], P('fsdp', 'seq'), may hold values from -6 to 6
Outputs:
- owner_output: bfloat16 [8, 8192, 1536], P('fsdp', 'seq')
- frame_grad: bfloat16 [8, 4096, 1536], P('fsdp', 'seq')
- w_grad: float32 [1536, 3072], P(('seq', 'fsdp'))
Inputs may be any that keep to these rules, and one draw needn't show every extreme that they name: Row g: device i of seq owns the frames offsets[g, i] to offsets[g, i + 1] - 1; offsets[g, 0] = 0 and offsets[g, 32] = 4096; each device owns 128 // 4 to 256 frames, beginning within 64 of i * 128; in every group one device owns exactly 256. `lengths`: each row sums to 4096; its largest entry is exactly 2048.
All inputs are finite; a program needn't handle non-finite values.
Results may differ from a plain program's by a relative error of at most 0.025.
Values may be sent and summed in bfloat16 or wider, within the bound.
No kernel may reach another device: no remote copies, remote signals or barrier semaphores. Data moves between devices by JAX's collectives and lax.ppermute only.
A program may use at most 128 MiB of HBM per device.

v0:
```python
import math
import jax
import jax.numpy as jnp
from jax import lax
from jax.sharding import PartitionSpec as P

epsilon = 1e-05


def passed_along(value, axis, steps):
    count = lax.axis_size(axis)
    initial, last = (max(0, -steps), min(count, count - steps))
    return lax.ppermute(value, axis, [(source, source + steps) for source in range(initial, last)])


def normalize_rows(values):
    values = values.astype(jnp.float32)
    center = jnp.mean(values, axis=-1, keepdims=True)
    shifted = values - center
    scale_inv = lax.rsqrt(jnp.mean(shifted * shifted, axis=-1, keepdims=True) + epsilon)
    return (shifted * scale_inv, scale_inv)


def norm_backward(upstream, normed, scale_inv):
    first_mean = jnp.mean(upstream, axis=-1, keepdims=True)
    second_mean = jnp.mean(upstream * normed, axis=-1, keepdims=True)
    return scale_inv * (upstream - first_mean - normed * second_mean)


def depthwise(window, kernel, labels, row_count):
    tap_count = kernel.shape[0]
    half_width = tap_count // 2
    centre = labels[half_width : half_width + row_count]
    result = jnp.zeros((row_count, kernel.shape[1]), jnp.float32)
    for tap_index in range(tap_count):
        same_utt = (labels[tap_index : tap_index + row_count] == centre).astype(jnp.float32)
        result = (
            result
            + kernel[tap_index]
            * window[tap_index : tap_index + row_count].astype(jnp.float32)
            * same_utt[:, None]
        )
    return result


def depthwise_back(window, kernel, labels, row_count):
    tap_count = kernel.shape[0]
    half_width = tap_count // 2
    centre = labels[half_width : half_width + row_count]
    result = jnp.zeros((row_count, kernel.shape[1]), jnp.float32)
    for tap_index in range(tap_count):
        tap_row = 2 * half_width - tap_index
        same_utt = (labels[tap_row : tap_row + row_count] == centre).astype(jnp.float32)
        result = (
            result + kernel[tap_index] * window[tap_row : tap_row + row_count] * same_utt[:, None]
        )
    return result


def finish(d_glu, values, gates, hidden, normed, scale_inv, backward_product):
    d_mixed = jnp.concatenate(
        [d_glu * gates, d_glu * values * gates * (1.0 - gates)], axis=1
    ).astype(jnp.bfloat16)
    d_hidden = backward_product(d_mixed)
    d_rows = norm_backward(d_hidden, normed, scale_inv).astype(jnp.bfloat16)
    partial_sum = lax.dot_general(
        hidden, d_mixed, (((0,), (0,)), ((), ())), preferred_element_type=jnp.float32
    )
    return (d_rows, partial_sum)


def on_device(frames, lengths, offsets, w_in, kernel, cotangent):
    rows_in = frames[0]
    per_device = rows_in.shape[0]
    model_width = rows_in.shape[1]
    capacity = 2 * per_device
    seq_count = lax.axis_size("seq")
    group_count = lax.axis_size("fsdp")
    device = lax.axis_index("seq")
    frame_total = seq_count * per_device
    half_width = kernel.shape[0] // 2
    bounds_row = offsets[0]
    start_row = bounds_row[device]
    owned_load = bounds_row[device + 1] - start_row
    base_row = (device - 1) * per_device
    utt_bounds = jnp.cumsum(lengths[0])[:-1]
    slot_index = jnp.arange(capacity, dtype=jnp.int32)
    owned = (slot_index < owned_load)[:, None]
    bf_zero = jnp.zeros((), jnp.bfloat16)
    cot_rows = jnp.where(owned, cotangent[0], bf_zero)

    def backward_product(d_mixed):
        return lax.dot_general(
            d_mixed,
            lax.all_gather(w_in, "fsdp", axis=0, tiled=True),
            (((1,), (1,)), ((), ())),
            preferred_element_type=jnp.float32,
        )

    from_prev = passed_along(rows_in, "seq", 1)
    from_next = passed_along(rows_in, "seq", -1)
    gathered = jnp.concatenate([from_prev, rows_in, from_next, jnp.zeros_like(rows_in)], axis=0)
    window_rows = capacity + 2 * half_width
    rows_window = lax.dynamic_slice_in_dim(
        gathered, start_row - half_width - base_row, window_rows, 0
    )
    positions = start_row - half_width + jnp.arange(window_rows, dtype=jnp.int32)
    labels = jnp.sum((positions[:, None] >= utt_bounds[None, :]).astype(jnp.int32), axis=1)
    inside = (positions >= 0) & (positions < frame_total)
    labels = jnp.where(inside, labels, -1)
    normed, scale_inv = normalize_rows(rows_window)
    hidden = normed.astype(jnp.bfloat16)
    projected = jnp.dot(
        hidden, lax.all_gather(w_in, "fsdp", axis=0, tiled=True), preferred_element_type=jnp.float32
    )
    values = projected[:, :model_width]
    gates = jax.nn.sigmoid(projected[:, model_width:])
    glu_out = (values * gates).astype(jnp.bfloat16)
    conv = depthwise(glu_out, kernel, labels, capacity)
    conv_normed, conv_inv = normalize_rows(conv)
    gate_out = jax.nn.sigmoid(conv_normed)
    output = conv_normed * gate_out
    owner_output = jnp.where(owned, output.astype(jnp.bfloat16), bf_zero)
    upstream = cot_rows.astype(jnp.float32)
    d_normed = upstream * (gate_out + output * (1.0 - gate_out))
    d_conv = jnp.where(owned, norm_backward(d_normed, conv_normed, conv_inv), 0.0)
    tail_rows = lax.dynamic_slice_in_dim(d_conv, owned_load - half_width, half_width, 0)
    head_rows = d_conv[:half_width]
    left_part = passed_along(tail_rows.astype(jnp.bfloat16), "seq", 1).astype(tail_rows.dtype)
    right_part = passed_along(head_rows.astype(jnp.bfloat16), "seq", -1).astype(head_rows.dtype)
    edge_zeros = jnp.zeros((half_width, model_width), jnp.float32)
    d_window = jnp.concatenate([left_part, d_conv, edge_zeros], axis=0)
    right_placed = lax.dynamic_update_slice_in_dim(
        jnp.zeros((window_rows, model_width), jnp.float32), right_part, half_width + owned_load, 0
    )
    d_window = d_window + right_placed
    d_glu = jnp.where(owned, depthwise_back(d_window, kernel, labels, capacity), 0.0)
    inner_end = half_width + capacity
    d_rows, partial_sum = finish(
        d_glu,
        values[half_width:inner_end],
        gates[half_width:inner_end],
        hidden[half_width:inner_end],
        normed[half_width:inner_end],
        scale_inv[half_width:inner_end],
        backward_product,
    )
    placed = lax.dynamic_update_slice_in_dim(
        jnp.zeros((4 * per_device, model_width), jnp.bfloat16), d_rows, start_row - base_row, 0
    )
    back_prev = passed_along(placed[:per_device], "seq", -1)
    back_next = passed_along(placed[2 * per_device : 3 * per_device], "seq", 1)
    frame_grad = (
        placed[per_device : 2 * per_device].astype(jnp.float32)
        + back_prev.astype(jnp.float32)
        + back_next.astype(jnp.float32)
    ).astype(jnp.bfloat16)
    rounded = lax.optimization_barrier(partial_sum.astype(jnp.bfloat16)).astype(jnp.float32)
    seq_summed = lax.psum_scatter(
        rounded.astype(jnp.bfloat16), "seq", scatter_dimension=0, tiled=True
    )
    summed = lax.psum_scatter(seq_summed, "fsdp", scatter_dimension=0, tiled=True).astype(
        jnp.float32
    )
    w_grad = summed * (1.0 / math.sqrt(group_count * frame_total))
    return (owner_output[None], frame_grad[None], w_grad)


def solution(mesh):
    return jax.shard_map(
        on_device,
        mesh=mesh,
        in_specs=(
            P("fsdp", "seq", None),
            P("fsdp", None),
            P("fsdp", None),
            P("fsdp", None),
            P(),
            P("fsdp", "seq", None),
        ),
        out_specs=(P("fsdp", "seq", None), P("fsdp", "seq", None), P(("seq", "fsdp"), None)),
        check_vma=False,
    )
```

profile of v0, /device:TPU:8, one launch (start us, length us, event | category | flops | bytes accessed | tf_op | source)
XLA Modules:
  0.0 391.4 jit_solution(15712493318630391508)
XLA Ops:
  7.2 0.7 all-gather.2.cloned.1.call-update
  8.0 3.8 collective-permute-start
  11.8 1.3 collective-permute-start.1
  13.1 1.4 constant_dynamic-slice_fusion.1
  15.2 0.8 reduce-window.4
  17.6 1.6 slice_reduce_fusion.29
  19.6 0.6 compare_convert_fusion.28
  20.3 0.5 iota_compare_fusion
  20.8 1.8 slice_reduce_fusion.30
  22.7 0.7 compare_convert_fusion.27
  23.4 1.3 collective-permute-done.1
  24.7 0.9 convert_reduce_fusion
  25.6 0.4 fusion.3
  26.0 1.5 fusion.1
  27.6 41.1 %all-gather.2.cloned.1.call-done = bf16[1536,3072]{1,0:T(8,128)(2,1)} async-done(((bf16[192,3072]{1,0:T(8,128)(2,1)}), bf16[1536,3072]{1,0:T(8,128)(2,1)}) %all-gather.2.cloned.1.call-update) | async-done | bytes 9437200 | tf_op jit(solution)/shard_map/all_gather | solution.py:114
  68.7 5.4 %fusion.90 = f32[286,3072]{1,0:T(8,128)S(1)} fusion(bf16[286,1536]{1,0:T(8,128)(2,1)S(1)} %get-tuple-element.52, bf16[1536,3072]{1,0:T(8,128)(2,1)} %all-gather.2.cloned.1.call-done), kind=kOutput, calls=%fused_computation.223 | convolution fusion | flops 2699034624 | bytes 13830144 | tf_op jit(solution)/shard_map/dot_general | solution.py:113
  74.2 2.1 fusion.6
  76.9 13.3 %fusion.86 = (f32[256]{0:T(256)S(1)}, f32[256,1536]{1,0:T(8,128)S(1)}) fusion(f32[256]{0:T(256)S(1)} %get-tuple-element.82, bf16[286,1536]{1,0:T(8,128)(2,1)S(1)} %get-tuple-element.46, f32[1536]{0:T(1024)S(1)} %get-tuple-element.36, f32[256]{0:T(256)S(1)} %get-tuple-element.54, f32[1536]{0:T(1024)S(1)} %get-tuple-element.37, f32[256]{0:T(256)S(1)} %get-tuple-element.55, ...), kind=kLoop, calls=%fused_computation.220 | loop fusion | flops 48365312 | bytes 26174464 | tf_op jit(solution)/shard_map/reduce_sum | solution.py:18
  90.5 0.8 copy-done.7
  91.3 1.7 fusion.84
  93.0 1.1 multiply_select_fusion
  94.2 1.1 copy-done.2
  95.3 3.5 collective-permute-start.2
  98.8 0.7 pad.4.clone
  99.5 1.5 collective-permute-start.3
  101.0 1.6 maximum_maximum_fusion
  102.6 2.9 collective-permute-done.3
  105.5 0.8 add.319
  106.2 10.6 %multiply_convert_fusion.1 = (bf16[256,1536]{1,0:T(8,128)(2,1)S(1)}, f32[256,1536]{1,0:T(8,128)S(1)}) fusion(f32[286,1536]{1,0:T(8,128)} %get-tuple-element.45, f32[256]{0:T(256)} %copy-done.37, f32[286,1536]{1,0:T(8,128)S(1)} %add.319, f32[1536]{0:T(1024)} %copy-done.26, f32[256]{0:T(256)} %copy-done.46, f32[1536]{0:T(1024)} %copy-done.27, ...), kind=kLoop, calls=%fused_computation.115 | loop fusion | flops 36962304 | bytes 52912384 | tf_op jit(solution)/shard_map/convert
  116.9 2.3 fusion.10
  119.2 0.9 copy-done.8
  120.0 5.2 %convolution_convert_fusion = bf16[1536,3072]{1,0:T(8,128)(2,1)} fusion(bf16[256,1536]{1,0:T(8,128)(2,1)S(1)} %fusion.10, bf16[256,1536]{1,0:T(8,128)(2,1)S(1)} %get-tuple-element.38, bf16[286,1536]{1,0:T(8,128)(2,1)S(1)} %copy-done.6), kind=kOutput, calls=%fused_computation | convolution fusion | flops 2423783424 | bytes 11796480 | tf_op jit(solution)/shard_map/dot_general | solution.py:66
  126.1 0.6 dynamic-slice.8
  127.5 2.1 select_bitcast_fusion
  129.5 5.9 %fusion.83 = (f32[256]{0:T(256)S(1)}, f32[256]{0:T(256)S(1)}, f32[256,1536]{1,0:T(8,128)S(1)}) fusion(f32[286,1536]{1,0:T(8,128)S(1)} %copy-done.3, bf16[1536,3072]{1,0:T(8,128)(2,1)} %all-gather.2.cloned.1.call-done, bf16[256,1536]{1,0:T(8,128)(2,1)} %copy-done.8, bf16[256,1536]{1,0:T(8,128)(2,1)} %copy-done.9), kind=kOutput, calls=%fused_computation.218 | convolution fusion | flops 2420243968 | bytes 14157824 | tf_op jit(solution)/shard_map/dot_general | solution.py:93
  135.5 1.3 multiply_convert_fusion
  136.8 1.0 copy-done.4
  137.9 4.0 %dynamic_update_slice.7 = bf16[512,1536]{1,0:T(8,128)(2,1)S(1)} dynamic-update-slice(bf16[512,1536]{1,0:T(8,128)(2,1)S(1)} %broadcast_in_dim.45, bf16[256,1536]{1,0:T(8,128)(2,1)S(1)} %copy-done.4, s32[]{:T(128)S(6)} %select_n.46, s32[]{:T(128)} %constant.22.clone.1) | dynamic-update-slice | bytes 1572868 | tf_op jit(solution)/shard_map/dynamic_update_slice | solution.py:148
  141.9 1.3 collective-permute-start.4
  143.2 4.6 %collective-permute-start.5 = (bf16[128,1536]{1,0:T(8,128)(2,1)S(1)}, bf16[128,1536]{1,0:T(8,128)(2,1)S(1)}, u32[]{:S(2)}, u32[]{:S(2)}) collective-permute-start(bf16[128,1536]{1,0:T(8,128)(2,1)S(1)} %get-tuple-element.48), channel_id=1, source_target_pairs={{0,8},{8,16},{16,24},{24,32},{32,40},{40,48},{48,56},{56,64},{64,7... | collective-permute-start | bytes 1179656 | tf_op jit(solution)/shard_map/ppermute | solution.py:13
  147.8 212.4 %reduce-scatter.4.cloned.1.call-done = bf16[48,3072]{1,0:T(8,128)(2,1)} async-done(((bf16[1536,3072]{1,0:T(8,128)(2,1)}), bf16[48,3072]{1,0:T(8,128)(2,1)}) %reduce-scatter.4.cloned.1.call-update) | async-done | bytes 294928 | tf_op jit(solution)/shard_map/reduce_scatter | solution.py:159
  360.2 14.8 %fusion = bf16[8,3072]{1,0:T(8,128)(2,1)S(1)} fusion(bf16[48,3072]{1,0:T(8,128)(2,1)} %reduce-scatter.4.cloned.1.call-done), kind=kCustom, calls=%all-reduce-scatter | all-reduce-scatter fusion | flops 196609 | bytes 345088
  375.0 1.9 collective-permute-start.6
  376.9 2.1 collective-permute-start.7
  379.0 0.9 fusion.79
  379.9 3.6 collective-permute-done.7
  383.6 0.3 concatenate.16
  383.9 0.7 convert_multiply_fusion
  (136 shorter events, 1.6 us)
Async XLA Ops:
  7.2 17.5 %copy-start.10 = (bf16[1,128,1536]{2,1,0:T(8,128)(2,1)S(1)}, bf16[1,128,1536]{2,1,0:T(8,128)(2,1)}, u32[]{:S(2)}) copy-start(bf16[1,128,1536]{2,1,0:T(8,128)(2,1)} %param.6) | copy-start | bytes 1179652
  7.2 61.5 %all-gather.2.cloned.1.call-start = ((), (), s32[]{:S(2)}) async-start(), calls=%async_computation.1 | async-start | bytes 10616832 | tf_op jit(solution)/shard_map/all_gather | solution.py:114
  7.9 352.3 %reduce-scatter.4.cloned.1.call-start = ((), (), s32[]{:S(2)}) async-start(), calls=%async_computation.2 | async-start | bytes 9732096 | tf_op jit(solution)/shard_map/reduce_scatter | solution.py:159
  8.0 15.4 %collective-permute-start = (bf16[128,1536]{1,0:T(8,128)(2,1)}, bf16[128,1536]{1,0:T(8,128)(2,1)S(1)}, u32[]{:S(2)}, u32[]{:S(2)}) collective-permute-start(bf16[128,1536]{1,0:T(8,128)(2,1)} %bitcast.21), channel_id=1, source_target_pairs={{0,8},{8,16},{16,24},{24,32},{32,40},{40,48},{48,56},{56,64},{64,7... | collective-permute-start | bytes 1179656 | tf_op jit(solution)/shard_map/ppermute | solution.py:13
  11.8 12.8 %collective-permute-start.1 = (bf16[128,1536]{1,0:T(8,128)(2,1)}, bf16[128,1536]{1,0:T(8,128)(2,1)S(1)}, u32[]{:S(2)}, u32[]{:S(2)}) collective-permute-start(bf16[128,1536]{1,0:T(8,128)(2,1)} %bitcast.22), channel_id=1, source_target_pairs={{8,0},{16,8},{24,16},{32,24},{40,32},{48,40},{56,48},{64,56},{72,6... | collective-permute-start | bytes 1179656 | tf_op jit(solution)/shard_map/ppermute | solution.py:13
  19.2 57.3 %copy-start.16 = (f32[1536]{0:T(1024)}, f32[1536]{0:T(1024)S(1)}, u32[]{:S(2)}) copy-start(f32[1536]{0:T(1024)S(1)} %get-tuple-element.26) | copy-start | bytes 18436
  19.2 57.3 %copy-start.17 = (f32[1536]{0:T(1024)}, f32[1536]{0:T(1024)S(1)}, u32[]{:S(2)}) copy-start(f32[1536]{0:T(1024)S(1)} %get-tuple-element.27) | copy-start | bytes 18436
  19.2 57.3 %copy-start.18 = (f32[1536]{0:T(1024)}, f32[1536]{0:T(1024)S(1)}, u32[]{:S(2)}) copy-start(f32[1536]{0:T(1024)S(1)} %get-tuple-element.28) | copy-start | bytes 18436
  19.2 57.3 %copy-start.19 = (f32[1536]{0:T(1024)}, f32[1536]{0:T(1024)S(1)}, u32[]{:S(2)}) copy-start(f32[1536]{0:T(1024)S(1)} %get-tuple-element.29) | copy-start | bytes 18436
  19.3 57.3 %copy-start.20 = (f32[1536]{0:T(1024)}, f32[1536]{0:T(1024)S(1)}, u32[]{:S(2)}) copy-start(f32[1536]{0:T(1024)S(1)} %get-tuple-element.30) | copy-start | bytes 18436
  19.3 57.3 %copy-start.21 = (f32[1536]{0:T(1024)}, f32[1536]{0:T(1024)S(1)}, u32[]{:S(2)}) copy-start(f32[1536]{0:T(1024)S(1)} %get-tuple-element.31) | copy-start | bytes 18436
  19.3 57.3 %copy-start.22 = (f32[1536]{0:T(1024)}, f32[1536]{0:T(1024)S(1)}, u32[]{:S(2)}) copy-start(f32[1536]{0:T(1024)S(1)} %get-tuple-element.32) | copy-start | bytes 18436
  19.3 57.3 %copy-start.23 = (f32[1536]{0:T(1024)}, f32[1536]{0:T(1024)S(1)}, u32[]{:S(2)}) copy-start(f32[1536]{0:T(1024)S(1)} %get-tuple-element.33) | copy-start | bytes 18436
  19.3 57.3 %copy-start.24 = (f32[1536]{0:T(1024)}, f32[1536]{0:T(1024)S(1)}, u32[]{:S(2)}) copy-start(f32[1536]{0:T(1024)S(1)} %get-tuple-element.34) | copy-start | bytes 18436
  19.3 57.3 %copy-start.25 = (f32[1536]{0:T(1024)}, f32[1536]{0:T(1024)S(1)}, u32[]{:S(2)}) copy-start(f32[1536]{0:T(1024)S(1)} %get-tuple-element.35) | copy-start | bytes 18436
  19.3 57.3 %copy-start.26 = (f32[1536]{0:T(1024)}, f32[1536]{0:T(1024)S(1)}, u32[]{:S(2)}) copy-start(f32[1536]{0:T(1024)S(1)} %get-tuple-element.36) | copy-start | bytes 18436
  19.3 57.3 %copy-start.27 = (f32[1536]{0:T(1024)}, f32[1536]{0:T(1024)S(1)}, u32[]{:S(2)}) copy-start(f32[1536]{0:T(1024)S(1)} %get-tuple-element.37) | copy-start | bytes 18436
  19.4 57.2 %copy-start.34 = (f32[256]{0:T(256)}, f32[256]{0:T(256)S(1)}, u32[]{:S(2)}) copy-start(f32[256]{0:T(256)S(1)} %get-tuple-element.80) | copy-start | bytes 3076
  19.4 57.2 %copy-start.35 = (f32[256]{0:T(256)}, f32[256]{0:T(256)S(1)}, u32[]{:S(2)}) copy-start(f32[256]{0:T(256)S(1)} %get-tuple-element.81) | copy-start | bytes 3076
  19.4 57.2 %copy-start.36 = (f32[256]{0:T(256)}, f32[256]{0:T(256)S(1)}, u32[]{:S(2)}) copy-start(f32[256]{0:T(256)S(1)} %get-tuple-element.82) | copy-start | bytes 3076
  19.5 57.2 %copy-start.37 = (f32[256]{0:T(256)}, f32[256]{0:T(256)S(1)}, u32[]{:S(2)}) copy-start(f32[256]{0:T(256)S(1)} %get-tuple-element.53) | copy-start | bytes 3076
  19.5 57.2 %copy-start.38 = (f32[256]{0:T(256)}, f32[256]{0:T(256)S(1)}, u32[]{:S(2)}) copy-start(f32[256]{0:T(256)S(1)} %get-tuple-element.54) | copy-start | bytes 3076
  19.5 57.2 %copy-start.39 = (f32[256]{0:T(256)}, f32[256]{0:T(256)S(1)}, u32[]{:S(2)}) copy-start(f32[256]{0:T(256)S(1)} %get-tuple-element.55) | copy-start | bytes 3076
  19.5 57.2 %copy-start.40 = (f32[256]{0:T(256)}, f32[256]{0:T(256)S(1)}, u32[]{:S(2)}) copy-start(f32[256]{0:T(256)S(1)} %get-tuple-element.56) | copy-start | bytes 3076
  19.6 57.2 %copy-start.41 = (f32[256]{0:T(256)}, f32[256]{0:T(256)S(1)}, u32[]{:S(2)}) copy-start(f32[256]{0:T(256)S(1)} %get-tuple-element.57) | copy-start | bytes 3076
  19.6 57.2 %copy-start.42 = (f32[256]{0:T(256)}, f32[256]{0:T(256)S(1)}, u32[]{:S(2)}) copy-start(f32[256]{0:T(256)S(1)} %get-tuple-element.58) | copy-start | bytes 3076
  19.6 57.2 %copy-start.43 = (f32[256]{0:T(256)}, f32[256]{0:T(256)S(1)}, u32[]{:S(2)}) copy-start(f32[256]{0:T(256)S(1)} %get-tuple-element.59) | copy-start | bytes 3076
  19.6 57.2 %copy-start.44 = (f32[256]{0:T(256)}, f32[256]{0:T(256)S(1)}, u32[]{:S(2)}) copy-start(f32[256]{0:T(256)S(1)} %get-tuple-element.60) | copy-start | bytes 3076
  19.6 57.2 %copy-start.45 = (f32[256]{0:T(256)}, f32[256]{0:T(256)S(1)}, u32[]{:S(2)}) copy-start(f32[256]{0:T(256)S(1)} %get-tuple-element.61) | copy-start | bytes 3076
  20.2 56.5 %copy-start.46 = (f32[256]{0:T(256)}, f32[256]{0:T(256)S(1)}, u32[]{:S(2)}) copy-start(f32[256]{0:T(256)S(1)} %get-tuple-element.62) | copy-start | bytes 3076
  20.2 56.5 %copy-start.47 = (f32[256]{0:T(256)}, f32[256]{0:T(256)S(1)}, u32[]{:S(2)}) copy-start(f32[256]{0:T(256)S(1)} %get-tuple-element.63) | copy-start | bytes 3076
  20.2 56.5 %copy-start.48 = (f32[256]{0:T(256)}, f32[256]{0:T(256)S(1)}, u32[]{:S(2)}) copy-start(f32[256]{0:T(256)S(1)} %get-tuple-element.64) | copy-start | bytes 3076
  20.2 56.6 %copy-start.49 = (f32[256]{0:T(256)}, f32[256]{0:T(256)S(1)}, u32[]{:S(2)}) copy-start(f32[256]{0:T(256)S(1)} %get-tuple-element.65) | copy-start | bytes 3076
  20.2 56.6 %copy-start.50 = (f32[256]{0:T(256)}, f32[256]{0:T(256)S(1)}, u32[]{:S(2)}) copy-start(f32[256]{0:T(256)S(1)} %get-tuple-element.66) | copy-start | bytes 3076
  20.2 56.6 %copy-start.51 = (f32[256]{0:T(256)}, f32[256]{0:T(256)S(1)}, u32[]{:S(2)}) copy-start(f32[256]{0:T(256)S(1)} %get-tuple-element.67) | copy-start | bytes 3076
  20.3 56.6 %copy-start.52 = (f32[256]{0:T(256)}, f32[256]{0:T(256)S(1)}, u32[]{:S(2)}) copy-start(f32[256]{0:T(256)S(1)} %get-tuple-element.68) | copy-start | bytes 3076
  22.6 54.2 %copy-start.11 = (f32[1536]{0:T(1024)}, f32[1536]{0:T(1024)S(1)}, u32[]{:S(2)}) copy-start(f32[1536]{0:T(1024)S(1)} %get-tuple-element.21) | copy-start | bytes 18436
  22.6 54.2 %copy-start.12 = (f32[1536]{0:T(1024)}, f32[1536]{0:T(1024)S(1)}, u32[]{:S(2)}) copy-start(f32[1536]{0:T(1024)S(1)} %get-tuple-element.22) | copy-start | bytes 18436
  22.6 54.2 %copy-start.13 = (f32[1536]{0:T(1024)}, f32[1536]{0:T(1024)S(1)}, u32[]{:S(2)}) copy-start(f32[1536]{0:T(1024)S(1)} %get-tuple-element.23) | copy-start | bytes 18436
  22.6 54.2 %copy-start.14 = (f32[1536]{0:T(1024)}, f32[1536]{0:T(1024)S(1)}, u32[]{:S(2)}) copy-start(f32[1536]{0:T(1024)S(1)} %get-tuple-element.24) | copy-start | bytes 18436
  22.7 54.2 %copy-start.15 = (f32[1536]{0:T(1024)}, f32[1536]{0:T(1024)S(1)}, u32[]{:S(2)}) copy-start(f32[1536]{0:T(1024)S(1)} %get-tuple-element.25) | copy-start | bytes 18436
  27.5 46.6 %copy-start.5 = (bf16[286,1536]{1,0:T(8,128)(2,1)}, bf16[286,1536]{1,0:T(8,128)(2,1)S(1)}, u32[]{:S(2)}) copy-start(bf16[286,1536]{1,0:T(8,128)(2,1)S(1)} %get-tuple-element.52) | copy-start | bytes 2635780
  95.3 5.6 %collective-permute-start.2 = (bf16[15,1536]{1,0:T(8,128)(2,1)S(1)}, bf16[15,1536]{1,0:T(8,128)(2,1)S(1)}, u32[]{:S(2)}, u32[]{:S(2)}) collective-permute-start(bf16[15,1536]{1,0:T(8,128)(2,1)S(1)} %get-tuple-element.50), channel_id=1, source_target_pairs={{0,8},{8,16},{16,24},{24,32},{32,40},{40,48},{48,56},{56,64},{64,7... | collective-permute-start | bytes 138248 | tf_op jit(solution)/shard_map/ppermute | solution.py:13
  99.5 6.0 %collective-permute-start.3 = (bf16[15,1536]{1,0:T(8,128)(2,1)S(1)}, bf16[15,1536]{1,0:T(8,128)(2,1)S(1)}, u32[]{:S(2)}, u32[]{:S(2)}) collective-permute-start(bf16[15,1536]{1,0:T(8,128)(2,1)S(1)} %get-tuple-element.49), channel_id=1, source_target_pairs={{8,0},{16,8},{24,16},{32,24},{40,32},{48,40},{56,48},{64,56},{72,6... | collective-permute-start | bytes 138248 | tf_op jit(solution)/shard_map/ppermute | solution.py:13
  141.9 237.1 %collective-permute-start.4 = (bf16[128,1536]{1,0:T(8,128)(2,1)S(1)}, bf16[128,1536]{1,0:T(8,128)(2,1)S(1)}, u32[]{:S(2)}, u32[]{:S(2)}) collective-permute-start(bf16[128,1536]{1,0:T(8,128)(2,1)S(1)} %get-tuple-element.47), channel_id=1, source_target_pairs={{8,0},{16,8},{24,16},{32,24},{40,32},{48,40},{56,48},{64,56},{72,6... | collective-permute-start | bytes 1179656 | tf_op jit(solution)/shard_map/ppermute | solution.py:13
  143.2 235.8 %collective-permute-start.5 = (bf16[128,1536]{1,0:T(8,128)(2,1)S(1)}, bf16[128,1536]{1,0:T(8,128)(2,1)S(1)}, u32[]{:S(2)}, u32[]{:S(2)}) collective-permute-start(bf16[128,1536]{1,0:T(8,128)(2,1)S(1)} %get-tuple-element.48), channel_id=1, source_target_pairs={{0,8},{8,16},{16,24},{24,32},{32,40},{40,48},{48,56},{56,64},{64,7... | collective-permute-start | bytes 1179656 | tf_op jit(solution)/shard_map/ppermute | solution.py:13
  375.0 8.5 %collective-permute-start.6 = (bf16[8,3072]{1,0:T(8,128)(2,1)S(1)}, bf16[8,3072]{1,0:T(8,128)(2,1)S(1)}, u32[]{:S(2)}, u32[]{:S(2)}) collective-permute-start(bf16[8,3072]{1,0:T(8,128)(2,1)S(1)} %fusion), channel_id=1, source_target_pairs={{0,1},{1,2},{2,3},{3,4},{4,5},{5,6},{6,7},{8,9},{9,10},{10,11},{11... | collective-permute-start | bytes 147464
  376.9 6.6 %collective-permute-start.7 = (bf16[6,3072]{1,0:T(8,128)(2,1)S(1)}, bf16[6,3072]{1,0:T(8,128)(2,1)S(1)}, u32[]{:S(2)}, u32[]{:S(2)}) collective-permute-start(bf16[6,3072]{1,0:T(8,128)(2,1)S(1)} %slice.684), channel_id=1, source_target_pairs={{0,2},{1,3},{2,4},{3,5},{4,6},{5,7},{8,10},{9,11},{10,12},{11,13},... | collective-permute-start | bytes 110600
  (16 other events, 40.5 us)
Sparse Core Ops, SparseCore 0:
  9.8 58.8 all-gather.1
  125.4 234.7 reduce-scatter.3
where the time goes:
time: 392 us; the launch traced here: 391 us
  waiting for transfers between devices  262 us (67%)
  other arithmetic  43.6 us (11%)
  starting transfers between devices  20 us (5%)
  between operations  18.5 us (5%)
  matrix products  16.6 us (4%)
  local copies, waits for them, and re-layouts  15.9 us (4%)
  blocking collectives  14.8 us (4%)
    reduce_scatter x1, waiting for transfers between devices, on_device(): lax.psum_scatter(rounded.astype(jnp.bfloat16), 'seq', scatter_dimension=0...  212 us
    all_gather x1, waiting for transfers between devices, on_device(): lax.all_gather(w_in, 'fsdp', axis=0, tiled=True)  41.1 us
    ppermute x6, starting transfers between devices, passed_along(): lax.ppermute(value, axis, [(source, source + steps) for source in range(i...  15.9 us
    unnamed x1, blocking collectives  14.8 us
    reduce_sum x2, other arithmetic, normalize_rows(): center = jnp.mean(values, axis=-1, keepdims=True)  14.2 us
    another operation x3, other arithmetic  13.7 us
  transfers between devices with their start and end apart: 10, of which 5 were waited for; matrix products, arithmetic and copies ran while one was open for 11% of the time, Pallas kernels for 0%

commit v1 on v0

--- a/solution.py
+++ b/solution.py
@@ -1,3 +1,4 @@
+import functools
 import math
 import jax
 import jax.numpy as jnp
@@ -5,6 +6,22 @@
 from jax.sharding import PartitionSpec as P
 
 epsilon = 1e-05
+
+
+def name_pools(local_array, mesh_dim, dimension_no):
+    built = jnp.concatenate(
+        lax.all_to_all(
+            jnp.stack([local_array for _ in range(lax.axis_size(mesh_dim))]),
+            mesh_dim,
+            split_axis=0,
+            concat_axis=0,
+        ),
+        axis=dimension_no,
+    )
+    return built
+
+
+run_balance = functools.partial(name_pools, mesh_dim="fsdp", dimension_no=0)
 
 
 def passed_along(value, axis, steps):
@@ -110,9 +127,7 @@
     labels = jnp.where(inside, labels, -1)
     normed, scale_inv = normalize_rows(rows_window)
     hidden = normed.astype(jnp.bfloat16)
-    projected = jnp.dot(
-        hidden, lax.all_gather(w_in, "fsdp", axis=0, tiled=True), preferred_element_type=jnp.float32
-    )
+    projected = jnp.dot(hidden, run_balance(w_in), preferred_element_type=jnp.float32)
     values = projected[:, :model_width]
     gates = jax.nn.sigmoid(projected[:, model_width:])
     glu_out = (values * gates).astype(jnp.bfloat16)

time: 392 us -> 487 us (1.24)
  waiting for transfers between devices: 262 us -> 350 us
    all_to_all x0 -> x1, waiting for transfers between devices: none -> 124 us  [name_pools(): lax.all_to_all(jnp.stack([local_array for _ in range(lax.axis_size(mesh_d...]
    all_gather x1, waiting for transfers between devices: 41.1 us -> 0.01 us  [backward_product(): lax.all_gather(w_in, 'fsdp', axis=0, tiled=True)]
    all_to_all x0 -> x1, starting transfers between devices: none -> 7.24 us  [name_pools(): lax.all_to_all(jnp.stack([local_array for _ in range(lax.axis_size(mesh_d...]
    another operation x0 -> x1, local copies, waits for them, and re-layouts: none -> 6.19 us  [name_pools(): jnp.stack([local_array for _ in range(lax.axis_size(mesh_dim))])]
  transfers between devices with their start and end apart: 10 -> 11, of which waited for: 5 -> 6; matrix products, arithmetic and copies ran while one was open for 11% -> 17% of each run, Pallas kernels for 0% -> 0%
where the time goes in v1:
time: 487 us
  waiting for transfers between devices  350 us (72%)
  other arithmetic  43.1 us (9%)
  starting transfers between devices  24.2 us (5%)
  between operations  19.8 us (4%)
  local copies, waits for them, and re-layouts  18.4 us (4%)
  matrix products  16.6 us (3%)
  blocking collectives  14.7 us (3%)
    reduce_scatter x1, waiting for transfers between devices, on_device(): lax.psum_scatter(rounded.astype(jnp.bfloat16), 'seq', scatter_dimension=0...  213 us
    all_to_all x1, waiting for transfers between devices, name_pools(): lax.all_to_all(jnp.stack([local_array for _ in range(lax.axis_size(mesh_d...  124 us
    unnamed x1, blocking collectives  14.7 us
    reduce_sum x2, other arithmetic, normalize_rows(): center = jnp.mean(values, axis=-1, keepdims=True)  14.2 us
    another operation x3, other arithmetic  13 us
    ppermute x6, starting transfers between devices, passed_along(): lax.ppermute(value, axis, [(source, source + steps) for source in range(i...  12.8 us
  transfers between devices with their start and end apart: 11, of which 6 were waited for; matrix products, arithmetic and copies ran while one was open for 17% of the time, Pallas kernels for 0%

profile of v1, /device:TPU:8, one launch (start us, length us, event | category | flops | bytes accessed | tf_op | source)
XLA Modules:
  0.0 486.7 jit_solution(5899099318138466437)
XLA Ops:
  8.0 6.2 %stack.2 = bf16[8,192,3072]{2,1,0:T(8,128)(2,1)} broadcast(bf16[192,3072]{1,0:T(8,128)(2,1)} %param.9), dimensions={1,2} | broadcast | bytes 10616832 | tf_op jit(solution)/shard_map/stack | solution.py:14
  14.2 7.2 %all-to-all-start = ((bf16[8,192,3072]{2,1,0:T(8,128)(2,1)}), bf16[8,192,3072]{2,1,0:T(8,128)(2,1)}, u32[]{:S(2)}, u32[]{:S(2)}) async-start(bf16[8,192,3072]{2,1,0:T(8,128)(2,1)} %stack.2), calls=%async_computation | async-start | bytes 18874368 | tf_op jit(solution)/shard_map/all_to_all | solution.py:13
  21.4 0.7 all-gather.2.cloned.1.call-update
  22.2 2.1 collective-permute-start
  24.3 1.3 collective-permute-start.1
  25.6 0.7 constant_dynamic-slice_fusion.1
  29.2 0.7 compare_convert_fusion.28
  29.9 0.5 iota_compare_fusion
  30.8 0.7 compare_convert_fusion.27
  31.5 1.5 collective-permute-done
  33.0 4.3 collective-permute-done.1
  37.3 0.9 convert_reduce_fusion
  38.2 0.4 fusion.3
  38.6 1.6 fusion.1
  40.2 123.7 %all-to-all-done = bf16[8,192,3072]{2,1,0:T(8,128)(2,1)} async-done(((bf16[8,192,3072]{2,1,0:T(8,128)(2,1)}), bf16[8,192,3072]{2,1,0:T(8,128)(2,1)}, u32[]{:S(2)}, u32[]{:S(2)}) %all-to-all-start) | async-done | bytes 9437216 | tf_op jit(solution)/shard_map/all_to_all | solution.py:13
  163.9 5.4 %fusion.90 = f32[286,3072]{1,0:T(8,128)S(1)} fusion(bf16[286,1536]{1,0:T(8,128)(2,1)S(1)} %get-tuple-element.52, bf16[1536,3072]{1,0:T(8,128)(2,1)} %bitcast.3), kind=kOutput, calls=%fused_computation.223 | convolution fusion | flops 2699034624 | bytes 13830144 | tf_op jit(solution)/shard_map/dot_general | solution.py:130
  169.3 2.1 fusion.6
  172.1 13.3 %fusion.86 = (f32[256]{0:T(256)S(1)}, f32[256,1536]{1,0:T(8,128)S(1)}) fusion(f32[256]{0:T(256)S(1)} %get-tuple-element.82, bf16[286,1536]{1,0:T(8,128)(2,1)S(1)} %get-tuple-element.46, f32[1536]{0:T(1024)S(1)} %get-tuple-element.36, f32[256]{0:T(256)S(1)} %get-tuple-element.54, f32[1536]{0:T(1024)S(1)} %get-tuple-element.37, f32[256]{0:T(256)S(1)} %get-tuple-element.55, ...), kind=kLoop, calls=%fused_computation.220 | loop fusion | flops 48365312 | bytes 26174464 | tf_op jit(solution)/shard_map/reduce_sum | solution.py:35
  185.7 0.8 copy-done.7
  186.5 1.7 fusion.84
  188.2 1.1 multiply_select_fusion
  189.4 1.1 copy-done.2
  190.5 2.1 collective-permute-start.2
  192.7 0.7 pad.4.clone
  193.3 1.5 collective-permute-start.3
  194.8 1.6 maximum_maximum_fusion
  196.4 2.9 collective-permute-done.3
  199.3 0.8 add.319
  200.1 10.6 %multiply_convert_fusion.1 = (bf16[256,1536]{1,0:T(8,128)(2,1)S(1)}, f32[256,1536]{1,0:T(8,128)S(1)}) fusion(f32[286,1536]{1,0:T(8,128)} %get-tuple-element.45, f32[256]{0:T(256)} %copy-done.38, f32[286,1536]{1,0:T(8,128)S(1)} %add.319, f32[1536]{0:T(1024)} %copy-done.27, f32[256]{0:T(256)} %copy-done.47, f32[1536]{0:T(1024)} %copy-done.28, ...), kind=kLoop, calls=%fused_computation.115 | loop fusion | flops 36962304 | bytes 52912384 | tf_op jit(solution)/shard_map/convert
  210.7 2.3 fusion.10
  213.0 0.9 copy-done.8
  213.9 5.2 %convolution_convert_fusion = bf16[1536,3072]{1,0:T(8,128)(2,1)} fusion(bf16[256,1536]{1,0:T(8,128)(2,1)S(1)} %fusion.10, bf16[256,1536]{1,0:T(8,128)(2,1)S(1)} %get-tuple-element.38, bf16[286,1536]{1,0:T(8,128)(2,1)S(1)} %copy-done.6), kind=kOutput, calls=%fused_computation | convolution fusion | flops 2423783424 | bytes 11796480 | tf_op jit(solution)/shard_map/dot_general | solution.py:83
  219.9 0.6 dynamic-slice.8
  221.2 2.1 select_bitcast_fusion
  223.3 5.9 %fusion.83 = (f32[256]{0:T(256)S(1)}, f32[256]{0:T(256)S(1)}, f32[256,1536]{1,0:T(8,128)S(1)}) fusion(f32[286,1536]{1,0:T(8,128)S(1)} %copy-done.3, bf16[1536,3072]{1,0:T(8,128)(2,1)} %all-gather.2.cloned.1.call-done, bf16[256,1536]{1,0:T(8,128)(2,1)} %copy-done.8, bf16[256,1536]{1,0:T(8,128)(2,1)} %copy-done.9), kind=kOutput, calls=%fused_computation.218 | convolution fusion | flops 2420243968 | bytes 14157824 | tf_op jit(solution)/shard_map/dot_general | solution.py:110
  229.2 1.3 multiply_convert_fusion
  230.6 1.0 copy-done.4
  231.7 4.0 dynamic_update_slice.7
  235.7 1.3 collective-permute-start.4
  237.0 4.6 collective-permute-start.5
  241.6 213.4 %reduce-scatter.4.cloned.1.call-done = bf16[48,3072]{1,0:T(8,128)(2,1)} async-done(((bf16[1536,3072]{1,0:T(8,128)(2,1)}), bf16[48,3072]{1,0:T(8,128)(2,1)}) %reduce-scatter.4.cloned.1.call-update) | async-done | bytes 294928 | tf_op jit(solution)/shard_map/reduce_scatter | solution.py:174
  455.0 14.7 %fusion = bf16[8,3072]{1,0:T(8,128)(2,1)S(1)} fusion(bf16[48,3072]{1,0:T(8,128)(2,1)} %reduce-scatter.4.cloned.1.call-done), kind=kCustom, calls=%all-reduce-scatter | all-reduce-scatter fusion | flops 196609 | bytes 345088
  469.7 1.9 collective-permute-start.6
  471.6 2.2 collective-permute-start.7
  473.8 0.9 fusion.79
  474.7 3.5 collective-permute-done.7
  478.2 0.3 concatenate.16
  478.6 0.7 convert_multiply_fusion
  (145 shorter events, 2.3 us)
Async XLA Ops:
  14.2 149.7 %all-to-all-start = ((bf16[8,192,3072]{2,1,0:T(8,128)(2,1)}), bf16[8,192,3072]{2,1,0:T(8,128)(2,1)}, u32[]{:S(2)}, u32[]{:S(2)}) async-start(bf16[8,192,3072]{2,1,0:T(8,128)(2,1)} %stack.2), calls=%async_computation | async-start | bytes 18874368 | tf_op jit(solution)/shard_map/all_to_all | solution.py:13
  21.4 201.9 %all-gather.2.cloned.1.call-start = ((), (), s32[]{:S(2)}) async-start(), calls=%async_computation.2 | async-start | bytes 10616832 | tf_op jit(solution)/shard_map/all_gather | solution.py:112
  22.2 432.8 %reduce-scatter.4.cloned.1.call-start = ((), (), s32[]{:S(2)}) async-start(), calls=%async_computation.3 | async-start | bytes 9732096 | tf_op jit(solution)/shard_map/reduce_scatter | solution.py:174
  22.2 10.8 %collective-permute-start = (bf16[128,1536]{1,0:T(8,128)(2,1)S(1)}, bf16[128,1536]{1,0:T(8,128)(2,1)S(1)}, u32[]{:S(2)}, u32[]{:S(2)}) collective-permute-start(bf16[128,1536]{1,0:T(8,128)(2,1)S(1)} %bitcast.22), channel_id=1, source_target_pairs={{0,8},{8,16},{16,24},{24,32},{32,40},{40,48},{48,56},{56,64},{64,7... | collective-permute-start | bytes 1179656 | tf_op jit(solution)/shard_map/ppermute | solution.py:30
  24.3 12.9 %collective-permute-start.1 = (bf16[128,1536]{1,0:T(8,128)(2,1)S(1)}, bf16[128,1536]{1,0:T(8,128)(2,1)S(1)}, u32[]{:S(2)}, u32[]{:S(2)}) collective-permute-start(bf16[128,1536]{1,0:T(8,128)(2,1)S(1)} %bitcast.23), channel_id=1, source_target_pairs={{8,0},{16,8},{24,16},{32,24},{40,32},{48,40},{56,48},{64,56},{72,6... | collective-permute-start | bytes 1179656 | tf_op jit(solution)/shard_map/ppermute | solution.py:30
  28.8 142.9 %copy-start.17 = (f32[1536]{0:T(1024)}, f32[1536]{0:T(1024)S(1)}, u32[]{:S(2)}) copy-start(f32[1536]{0:T(1024)S(1)} %get-tuple-element.26) | copy-start | bytes 18436
  28.8 142.9 %copy-start.18 = (f32[1536]{0:T(1024)}, f32[1536]{0:T(1024)S(1)}, u32[]{:S(2)}) copy-start(f32[1536]{0:T(1024)S(1)} %get-tuple-element.27) | copy-start | bytes 18436
  28.8 142.9 %copy-start.19 = (f32[1536]{0:T(1024)}, f32[1536]{0:T(1024)S(1)}, u32[]{:S(2)}) copy-start(f32[1536]{0:T(1024)S(1)} %get-tuple-element.28) | copy-start | bytes 18436
  28.8 142.9 %copy-start.20 = (f32[1536]{0:T(1024)}, f32[1536]{0:T(1024)S(1)}, u32[]{:S(2)}) copy-start(f32[1536]{0:T(1024)S(1)} %get-tuple-element.29) | copy-start | bytes 18436
  28.8 142.9 %copy-start.21 = (f32[1536]{0:T(1024)}, f32[1536]{0:T(1024)S(1)}, u32[]{:S(2)}) copy-start(f32[1536]{0:T(1024)S(1)} %get-tuple-element.30) | copy-start | bytes 18436
  28.9 142.9 %copy-start.22 = (f32[1536]{0:T(1024)}, f32[1536]{0:T(1024)S(1)}, u32[]{:S(2)}) copy-start(f32[1536]{0:T(1024)S(1)} %get-tuple-element.31) | copy-start | bytes 18436
  28.9 142.9 %copy-start.23 = (f32[1536]{0:T(1024)}, f32[1536]{0:T(1024)S(1)}, u32[]{:S(2)}) copy-start(f32[1536]{0:T(1024)S(1)} %get-tuple-element.32) | copy-start | bytes 18436
  28.9 142.9 %copy-start.24 = (f32[1536]{0:T(1024)}, f32[1536]{0:T(1024)S(1)}, u32[]{:S(2)}) copy-start(f32[1536]{0:T(1024)S(1)} %get-tuple-element.33) | copy-start | bytes 18436
  28.9 142.9 %copy-start.25 = (f32[1536]{0:T(1024)}, f32[1536]{0:T(1024)S(1)}, u32[]{:S(2)}) copy-start(f32[1536]{0:T(1024)S(1)} %get-tuple-element.34) | copy-start | bytes 18436
  28.9 142.9 %copy-start.26 = (f32[1536]{0:T(1024)}, f32[1536]{0:T(1024)S(1)}, u32[]{:S(2)}) copy-start(f32[1536]{0:T(1024)S(1)} %get-tuple-element.35) | copy-start | bytes 18436
  28.9 142.9 %copy-start.27 = (f32[1536]{0:T(1024)}, f32[1536]{0:T(1024)S(1)}, u32[]{:S(2)}) copy-start(f32[1536]{0:T(1024)S(1)} %get-tuple-element.36) | copy-start | bytes 18436
  28.9 142.9 %copy-start.28 = (f32[1536]{0:T(1024)}, f32[1536]{0:T(1024)S(1)}, u32[]{:S(2)}) copy-start(f32[1536]{0:T(1024)S(1)} %get-tuple-element.37) | copy-start | bytes 18436
  29.0 142.8 %copy-start.35 = (f32[256]{0:T(256)}, f32[256]{0:T(256)S(1)}, u32[]{:S(2)}) copy-start(f32[256]{0:T(256)S(1)} %get-tuple-element.80) | copy-start | bytes 3076
  29.0 142.8 %copy-start.36 = (f32[256]{0:T(256)}, f32[256]{0:T(256)S(1)}, u32[]{:S(2)}) copy-start(f32[256]{0:T(256)S(1)} %get-tuple-element.81) | copy-start | bytes 3076
  29.0 142.8 %copy-start.37 = (f32[256]{0:T(256)}, f32[256]{0:T(256)S(1)}, u32[]{:S(2)}) copy-start(f32[256]{0:T(256)S(1)} %get-tuple-element.82) | copy-start | bytes 3076
  29.1 142.8 %copy-start.38 = (f32[256]{0:T(256)}, f32[256]{0:T(256)S(1)}, u32[]{:S(2)}) copy-start(f32[256]{0:T(256)S(1)} %get-tuple-element.53) | copy-start | bytes 3076
  29.1 142.8 %copy-start.39 = (f32[256]{0:T(256)}, f32[256]{0:T(256)S(1)}, u32[]{:S(2)}) copy-start(f32[256]{0:T(256)S(1)} %get-tuple-element.54) | copy-start | bytes 3076
  29.1 142.8 %copy-start.40 = (f32[256]{0:T(256)}, f32[256]{0:T(256)S(1)}, u32[]{:S(2)}) copy-start(f32[256]{0:T(256)S(1)} %get-tuple-element.55) | copy-start | bytes 3076
  29.1 142.8 %copy-start.41 = (f32[256]{0:T(256)}, f32[256]{0:T(256)S(1)}, u32[]{:S(2)}) copy-start(f32[256]{0:T(256)S(1)} %get-tuple-element.56) | copy-start | bytes 3076
  29.1 142.8 %copy-start.42 = (f32[256]{0:T(256)}, f32[256]{0:T(256)S(1)}, u32[]{:S(2)}) copy-start(f32[256]{0:T(256)S(1)} %get-tuple-element.57) | copy-start | bytes 3076
  29.2 142.8 %copy-start.43 = (f32[256]{0:T(256)}, f32[256]{0:T(256)S(1)}, u32[]{:S(2)}) copy-start(f32[256]{0:T(256)S(1)} %get-tuple-element.58) | copy-start | bytes 3076
  29.2 142.8 %copy-start.44 = (f32[256]{0:T(256)}, f32[256]{0:T(256)S(1)}, u32[]{:S(2)}) copy-start(f32[256]{0:T(256)S(1)} %get-tuple-element.59) | copy-start | bytes 3076
  29.2 142.8 %copy-start.45 = (f32[256]{0:T(256)}, f32[256]{0:T(256)S(1)}, u32[]{:S(2)}) copy-start(f32[256]{0:T(256)S(1)} %get-tuple-element.60) | copy-start | bytes 3076
  29.2 142.8 %copy-start.46 = (f32[256]{0:T(256)}, f32[256]{0:T(256)S(1)}, u32[]{:S(2)}) copy-start(f32[256]{0:T(256)S(1)} %get-tuple-element.61) | copy-start | bytes 3076
  29.9 142.1 %copy-start.47 = (f32[256]{0:T(256)}, f32[256]{0:T(256)S(1)}, u32[]{:S(2)}) copy-start(f32[256]{0:T(256)S(1)} %get-tuple-element.62) | copy-start | bytes 3076
  29.9 142.1 %copy-start.48 = (f32[256]{0:T(256)}, f32[256]{0:T(256)S(1)}, u32[]{:S(2)}) copy-start(f32[256]{0:T(256)S(1)} %get-tuple-element.63) | copy-start | bytes 3076
  29.9 142.1 %copy-start.49 = (f32[256]{0:T(256)}, f32[256]{0:T(256)S(1)}, u32[]{:S(2)}) copy-start(f32[256]{0:T(256)S(1)} %get-tuple-element.64) | copy-start | bytes 3076
  29.9 142.1 %copy-start.50 = (f32[256]{0:T(256)}, f32[256]{0:T(256)S(1)}, u32[]{:S(2)}) copy-start(f32[256]{0:T(256)S(1)} %get-tuple-element.65) | copy-start | bytes 3076
  29.9 142.1 %copy-start.51 = (f32[256]{0:T(256)}, f32[256]{0:T(256)S(1)}, u32[]{:S(2)}) copy-start(f32[256]{0:T(256)S(1)} %get-tuple-element.66) | copy-start | bytes 3076
  29.9 142.1 %copy-start.52 = (f32[256]{0:T(256)}, f32[256]{0:T(256)S(1)}, u32[]{:S(2)}) copy-start(f32[256]{0:T(256)S(1)} %get-tuple-element.67) | copy-start | bytes 3076
  29.9 142.1 %copy-start.53 = (f32[256]{0:T(256)}, f32[256]{0:T(256)S(1)}, u32[]{:S(2)}) copy-start(f32[256]{0:T(256)S(1)} %get-tuple-element.68) | copy-start | bytes 3076
  30.7 141.3 %copy-start.12 = (f32[1536]{0:T(1024)}, f32[1536]{0:T(1024)S(1)}, u32[]{:S(2)}) copy-start(f32[1536]{0:T(1024)S(1)} %get-tuple-element.21) | copy-start | bytes 18436
  30.8 141.3 %copy-start.13 = (f32[1536]{0:T(1024)}, f32[1536]{0:T(1024)S(1)}, u32[]{:S(2)}) copy-start(f32[1536]{0:T(1024)S(1)} %get-tuple-element.22) | copy-start | bytes 18436
  30.8 141.3 %copy-start.14 = (f32[1536]{0:T(1024)}, f32[1536]{0:T(1024)S(1)}, u32[]{:S(2)}) copy-start(f32[1536]{0:T(1024)S(1)} %get-tuple-element.23) | copy-start | bytes 18436
  30.8 141.3 %copy-start.15 = (f32[1536]{0:T(1024)}, f32[1536]{0:T(1024)S(1)}, u32[]{:S(2)}) copy-start(f32[1536]{0:T(1024)S(1)} %get-tuple-element.24) | copy-start | bytes 18436
  30.8 141.3 %copy-start.16 = (f32[1536]{0:T(1024)}, f32[1536]{0:T(1024)S(1)}, u32[]{:S(2)}) copy-start(f32[1536]{0:T(1024)S(1)} %get-tuple-element.25) | copy-start | bytes 18436
  40.2 129.1 %copy-start.5 = (bf16[286,1536]{1,0:T(8,128)(2,1)}, bf16[286,1536]{1,0:T(8,128)(2,1)S(1)}, u32[]{:S(2)}) copy-start(bf16[286,1536]{1,0:T(8,128)(2,1)S(1)} %get-tuple-element.52) | copy-start | bytes 2635780
  190.5 4.2 collective-permute-start.2
  193.3 6.0 %collective-permute-start.3 = (bf16[15,1536]{1,0:T(8,128)(2,1)S(1)}, bf16[15,1536]{1,0:T(8,128)(2,1)S(1)}, u32[]{:S(2)}, u32[]{:S(2)}) collective-permute-start(bf16[15,1536]{1,0:T(8,128)(2,1)S(1)} %get-tuple-element.49), channel_id=1, source_target_pairs={{8,0},{16,8},{24,16},{32,24},{40,32},{48,40},{56,48},{64,56},{72,6... | collective-permute-start | bytes 138248 | tf_op jit(solution)/shard_map/ppermute | solution.py:30
  235.7 238.1 %collective-permute-start.4 = (bf16[128,1536]{1,0:T(8,128)(2,1)S(1)}, bf16[128,1536]{1,0:T(8,128)(2,1)S(1)}, u32[]{:S(2)}, u32[]{:S(2)}) collective-permute-start(bf16[128,1536]{1,0:T(8,128)(2,1)S(1)} %get-tuple-element.47), channel_id=1, source_target_pairs={{8,0},{16,8},{24,16},{32,24},{40,32},{48,40},{56,48},{64,56},{72,6... | collective-permute-start | bytes 1179656 | tf_op jit(solution)/shard_map/ppermute | solution.py:30
  237.0 236.8 %collective-permute-start.5 = (bf16[128,1536]{1,0:T(8,128)(2,1)S(1)}, bf16[128,1536]{1,0:T(8,128)(2,1)S(1)}, u32[]{:S(2)}, u32[]{:S(2)}) collective-permute-start(bf16[128,1536]{1,0:T(8,128)(2,1)S(1)} %get-tuple-element.48), channel_id=1, source_target_pairs={{0,8},{8,16},{16,24},{24,32},{32,40},{40,48},{48,56},{56,64},{64,7... | collective-permute-start | bytes 1179656 | tf_op jit(solution)/shard_map/ppermute | solution.py:30
  469.7 8.5 %collective-permute-start.6 = (bf16[8,3072]{1,0:T(8,128)(2,1)S(1)}, bf16[8,3072]{1,0:T(8,128)(2,1)S(1)}, u32[]{:S(2)}, u32[]{:S(2)}) collective-permute-start(bf16[8,3072]{1,0:T(8,128)(2,1)S(1)} %fusion), channel_id=1, source_target_pairs={{0,1},{1,2},{2,3},{3,4},{4,5},{5,6},{6,7},{8,9},{9,10},{10,11},{11... | collective-permute-start | bytes 147464
  471.6 6.6 %collective-permute-start.7 = (bf16[6,3072]{1,0:T(8,128)(2,1)S(1)}, bf16[6,3072]{1,0:T(8,128)(2,1)S(1)}, u32[]{:S(2)}, u32[]{:S(2)}) collective-permute-start(bf16[6,3072]{1,0:T(8,128)(2,1)S(1)} %slice.684), channel_id=1, source_target_pairs={{0,2},{1,3},{2,4},{3,5},{4,6},{5,7},{8,10},{9,11},{10,12},{11,13},... | collective-permute-start | bytes 110600
  (20 other events, 86.8 us)
Sparse Core Ops, SparseCore 0:
  24.1 106.8 all-gather.1
Sparse Core Ops, SparseCore 1:
  219.2 235.7 reduce-scatter.3
